TPU v7x, 32 devices: a whole 2x2x4 slice. The times are simulated.
32 devices in a mesh: phases: 2 (over x), tiles: 16 (over z, y, core).
Axes of the slice: x: 2, y: 2, z: 4, core: 2. Of those that a mesh axis runs over, the one named last changes fastest.
Arguments:
- kspace_grid: float32 [4, 32, 2, 64, 384], P('phases', 'tiles'), may hold values from -6 to 6
- samples: float32 [4, 128, 32, 128], P('phases', 'tiles'), may hold values from -6 to 6
- interp_matrix: bfloat16 [4, 16, 64, 384], P('phases', 'tiles'), may hold values from -0.3125 to 0.3125
- kernel_real: bfloat16 [5, 3, 32, 32], replicated, may hold values from -0.1875 to 0.1875
- kernel_imag: bfloat16 [5, 3, 32, 32], replicated, may hold values from -0.1875 to 0.1875
- segment_line: int32 [4, 16, 16, 2], P('phases', 'tiles'), may hold values from 0 to 3, as said below
- segment_readout: int32 [4, 16, 16, 2], P('phases', 'tiles'), may hold values from 0 to 7, as said below
- segment_count: int32 [4, 16, 16], P('phases', 'tiles'), may hold values from 0 to 2, as said below
Outputs:
- gradient: float32 [4, 32, 2, 64, 384], P('phases', 'tiles')
- data_residual: float32 [4, 128, 32, 128], P('phases', 'tiles')
Inputs may be any that keep to these rules, and one draw needn't show every extreme that they name: segment_count[p, t, o] slots, numbered from 0, are in use from tile t to owner o in phase p; every tile t with 8 - w <= t < 8 + w, w = max(2, 1), and in each phase one owner from every tile, have all 2 slots in use. `segment_line`: a line l of a tile stands for plane l // 2 and position l % 2 of that tile. `segment_readout`: readouts are numbered within their owner.
All inputs are finite; a program needn't handle non-finite values.
Results may differ from a plain program's by a relative error of at most 0.0029.
Values may be sent and summed in bfloat16 or wider, within the bound.
A program may use at most 64 MiB of HBM per device.

v0:
```python
import jax
import jax.numpy as jnp
from jax import lax
from jax.sharding import PartitionSpec as P

KX = 5
KZ = 3


SPIRIT_WEIGHT = 1.0
PHASE_WEIGHT = 0.15


def extended_2(block, sides, width):
    for axis, dim in sides:
        count = lax.axis_size(axis)
        forward = [(i, i + 1) for i in range(count - 1)]
        backward = [(target, source) for source, target in forward]
        low = lax.ppermute(
            lax.slice_in_dim(block, block.shape[dim] - width, None, axis=dim), axis, forward
        )
        high = lax.ppermute(lax.slice_in_dim(block, 0, width, axis=dim), axis, backward)
        block = jnp.concatenate([low, block, high], axis=dim)
    return block


def real_form(kernel_real, kernel_imag):
    upper_half = jnp.stack([kernel_real, -kernel_imag], axis=-1)
    lower_half = jnp.stack([kernel_imag, kernel_real], axis=-1)
    blocks = jnp.stack([upper_half, lower_half], axis=-3)
    block_shape = blocks.shape
    return blocks.reshape(block_shape[0], block_shape[1], block_shape[2] * 2, block_shape[4] * 2)


def stencil(extended, matrix, starts, planes, depth_z):
    results = []
    for phase_item in range(extended.shape[0]):
        single = extended[phase_item]
        shifted = [
            single[start_x : start_x + planes, :, :, start_z : start_z + depth_z]
            for start_x, start_z in starts
        ]
        stacked = jnp.stack(shifted, axis=2)
        stacked = stacked.reshape(planes, single.shape[1], -1, depth_z)
        results.append(
            jnp.einsum("ok,xykz->xyoz", matrix, stacked, preferred_element_type=jnp.float32)
        )
    return jnp.stack(results)


def widen_tiles(field_in, which):
    if which == 0:
        extended = extended_2(field_in, (("tiles", 1),), 2)
    else:
        extended = extended_2(field_in, (("tiles", 1),), 2)
    return jnp.pad(extended, ((0, 0), (0, 0), (0, 0), (0, 0), (1, 1)))


def pick_lines(line_table, line_index):
    return line_table[line_index]


def on_device(
    kspace_grid,
    samples,
    interp_matrix,
    kernel_real,
    kernel_imag,
    segment_line,
    segment_readout,
    segment_count,
):
    phase_here, planes, rows_y, channels, depth_z = kspace_grid.shape
    blocks = real_form(kernel_real, kernel_imag)
    forward_matrix = jnp.transpose(blocks, (2, 0, 1, 3)).reshape(channels, -1)
    adjoint_matrix = jnp.transpose(blocks, (3, 0, 1, 2)).reshape(channels, -1)
    forward_starts = [(tap_x, tap_z) for tap_x in range(KX) for tap_z in range(KZ)]
    adjoint_starts = [(4 - tap_x, 2 - tap_z) for tap_x in range(KX) for tap_z in range(KZ)]
    rounded = kspace_grid.astype(jnp.bfloat16)
    spirit = (
        stencil(widen_tiles(rounded, 0), forward_matrix, forward_starts, planes, depth_z)
        - kspace_grid
    )
    spirit_round = spirit.astype(jnp.bfloat16)
    adjoint = stencil(widen_tiles(spirit_round, 1), adjoint_matrix, adjoint_starts, planes, depth_z)
    tile_count = lax.axis_size("tiles")
    capacity = segment_line.shape[3]
    line_count = planes * rows_y
    segment_len = interp_matrix.shape[2]
    read_count = samples.shape[1]
    slot_live = (jnp.arange(capacity)[None, None, :] < segment_count[:, 0, :, None]).astype(
        jnp.float32
    )
    line_pick = segment_line[:, 0]
    readout_pick = segment_readout[:, 0]
    weights_here = interp_matrix[:, 0]
    grid_lines = rounded.reshape(phase_here, line_count, channels, depth_z)
    line_images = jnp.einsum(
        "plqz,psz->plqs", grid_lines, weights_here, preferred_element_type=jnp.float32
    )
    partial_value = jax.vmap(pick_lines)(line_images, line_pick)
    partial_value = partial_value * slot_live[..., None, None]
    partial_value = partial_value.reshape(
        phase_here, tile_count, capacity, channels // 2, 2 * segment_len
    )
    partial_value, readout_ids = (
        lax.all_to_all(partial_value, "tiles", split_axis=1, concat_axis=1, tiled=True),
        lax.all_to_all(readout_pick, "tiles", split_axis=1, concat_axis=1, tiled=True),
    )
    partial_value = partial_value.reshape(phase_here, tile_count, capacity, channels, segment_len)
    chooser = (readout_ids[..., None] == jnp.arange(read_count)).astype(jnp.float32)
    readings = jnp.einsum(
        "pncr,pncqs->prqs", chooser, partial_value, precision=lax.Precision.HIGHEST
    )
    data_residual = (
        readings.reshape(phase_here, read_count, channels // 2, 2 * segment_len) - samples
    )
    residual_round = data_residual.astype(jnp.bfloat16)
    residual_blocks = residual_round.reshape(phase_here, read_count, channels, segment_len)
    rows_back = jnp.einsum(
        "pncr,prqs->pncqs",
        chooser.astype(jnp.bfloat16),
        residual_blocks,
        preferred_element_type=jnp.float32,
    ).astype(jnp.bfloat16)
    returned = lax.all_to_all(rows_back, "tiles", split_axis=1, concat_axis=1, tiled=True)
    line_place = (
        (line_pick[..., None] == jnp.arange(line_count)).astype(jnp.float32) * slot_live[..., None]
    ).astype(jnp.bfloat16)
    line_rows = jnp.einsum(
        "pocl,pocqs->plqs", line_place, returned, preferred_element_type=jnp.float32
    )
    data_grad = jnp.einsum(
        "plqs,psz->plqz",
        line_rows,
        weights_here.astype(jnp.float32),
        precision=lax.Precision.HIGHEST,
    )
    data_grad = data_grad.reshape(phase_here, planes, rows_y, channels, depth_z)
    padded = extended_2(kspace_grid.astype(jnp.bfloat16), (("phases", 0),), 2).astype(
        kspace_grid.dtype
    )
    first_diff = padded[:-2] - 2.0 * padded[1:-1] + padded[2:]
    global_phase = lax.axis_index("phases") * phase_here + jnp.arange(phase_here + 2) - 1
    inside = ((global_phase >= 0) & (global_phase < lax.axis_size("phases") * phase_here)).astype(
        jnp.float32
    )
    first_diff = first_diff * inside[:, None, None, None, None]
    phase_bend = first_diff[:-2] - 2.0 * first_diff[1:-1] + first_diff[2:]
    gradient = data_grad + SPIRIT_WEIGHT * (adjoint - spirit) + PHASE_WEIGHT * phase_bend
    return (gradient, data_residual)


def solution(mesh):
    return jax.shard_map(
        on_device,
        mesh=mesh,
        in_specs=(
            P("phases", "tiles", None, None, None),
            P("phases", "tiles", None, None),
            P("phases", "tiles", None, None),
            P(),
            P(),
            P("phases", "tiles", None, None),
            P("phases", "tiles", None, None),
            P("phases", "tiles", None),
        ),
        out_specs=(P("phases", "tiles", None, None, None), P("phases", "tiles", None, None)),
        check_vma=False,
    )
```

profile of v0, /device:TPU:0, one launch (start us, length us, event | category | flops | bytes accessed | tf_op | source)
XLA Modules:
  0.0 136.9 jit_solution(10210122332051619298)
XLA Ops:
  0.6 2.0 %convert_element_type.52 = bf16[2,2,2,64,384]{4,3,2,1,0:T(8,128)(2,1)} convert(f32[2,2,2,64,384]{4,3,2,1,0:T(8,128)} %param.8) | non-fusion elementwise | flops 196608 | bytes 1179648 | tf_op jit(solution)/shard_map/convert_element_type | solution.py:79
  2.6 3.1 %collective-permute-start = (bf16[2,2,2,64,384]{4,3,2,1,0:T(8,128)(2,1)}, bf16[2,2,2,64,384]{4,3,2,1,0:T(8,128)(2,1)}, u32[]{:S(2)}, u32[]{:S(2)}) collective-permute-start(bf16[2,2,2,64,384]{4,3,2,1,0:T(8,128)(2,1)} %convert_element_type.52), channel_id=1, source_target_pairs={{0,1},{1,2},{2,3},{3,4},{4,5},{5,6},{6,7},{7,8},{8,9},{9,10},{10,1... | collective-permute-start | bytes 1179656 | tf_op jit(solution)/shard_map/ppermute | solution.py:19
  5.7 1.3 collective-permute-start.1
  7.0 5.0 %collective-permute-start.4 = (bf16[2,2,2,64,384]{4,3,2,1,0:T(8,128)(2,1)}, bf16[2,2,2,64,384]{4,3,2,1,0:T(8,128)(2,1)}, u32[]{:S(2)}, u32[]{:S(2)}) collective-permute-start(bf16[2,2,2,64,384]{4,3,2,1,0:T(8,128)(2,1)} %convert_element_type.52), channel_id=1, source_target_pairs={{0,16},{1,17},{2,18},{3,19},{4,20},{5,21},{6,22},{7,23},{8,24},{9,... | collective-permute-start | bytes 1179656 | tf_op jit(solution)/shard_map/ppermute | solution.py:19
  12.0 1.3 collective-permute-start.5
  13.3 1.4 copy.31
  14.7 7.7 %all-to-all-start = ((s32[2,16,2]{2,0,1:T(2,128)}), s32[2,16,2]{2,0,1:T(2,128)S(1)}, u32[]{:S(2)}, u32[]{:S(2)}) async-start(s32[2,16,2]{2,0,1:T(2,128)} %copy.31), calls=%async_computation | async-start | bytes 32768 | tf_op jit(solution)/shard_map/all_to_all | solution.py:108
  30.7 6.9 %copy.43 = bf16[5,3,32,2,32,2]{0,5,4,3,2,1:T(2,128)(2,1)S(1)} copy(bf16[5,3,32,2,32,2]{4,2,1,0,5,3:T(8,128)(2,1)} %pad_maximum_fusion) | data formatting | bytes 245760 | tf_op jit(solution)/shard_map/stack | solution.py:30
  37.6 4.2 %copy.44 = bf16[64,5,3,64]{0,3,2,1:T(8,128)(2,1)} copy(bf16[64,5,3,64]{1,3,0,2:T(8,128)(2,1)S(1)} %bitcast.351) | data formatting | bytes 245760 | tf_op jit(solution)/shard_map/transpose | solution.py:75
  41.9 1.9 %copy.49 = bf16[64,5,3,64]{0,3,2,1:T(8,128)(2,1)S(1)} copy(bf16[64,5,3,64]{1,0,3,2:T(8,128)(2,1)S(1)} %bitcast.352) | data formatting | bytes 245760 | tf_op jit(solution)/shard_map/transpose | solution.py:76
  43.8 6.1 %all-to-all-start.1 = ((f32[2,16,2,32,128]{4,3,2,0,1:T(8,128)}), f32[2,16,2,32,128]{4,3,2,0,1:T(8,128)}, u32[]{:S(2)}, u32[]{:S(2)}) async-start(f32[2,16,2,32,128]{4,3,2,0,1:T(8,128)} %copy_multiply_fusion), calls=%async_computation.1 | async-start | bytes 2097152 | tf_op jit(solution)/shard_map/all_to_all | solution.py:107
  49.9 2.2 %fusion.9 = bf16[2,6,2,64,386]{4,3,2,1,0:T(8,128)(2,1)S(1)} fusion(bf16[2,2,2,64,384]{4,3,2,1,0:T(8,128)(2,1)} %collective-permute-done.1, bf16[2,2,2,64,384]{4,3,2,1,0:T(8,128)(2,1)} %convert_element_type.52, bf16[2,2,2,64,384]{4,3,2,1,0:T(8,128)(2,1)} %collective-permute-done), kind=kLoop, calls=%fused_computation.16 | loop fusion | flops 7114752 | bytes 2365440 | tf_op jit(solution)/shard_map/concatenate | solution.py:23
  58.2 2.3 %collective-permute-start.2 = (bf16[2,2,2,64,384]{4,3,2,1,0:T(8,128)(2,1)S(1)}, bf16[2,2,2,64,384]{4,3,2,1,0:T(8,128)(2,1)S(1)}, u32[]{:S(2)}, u32[]{:S(2)}) collective-permute-start(bf16[2,2,2,64,384]{4,3,2,1,0:T(8,128)(2,1)S(1)} %fusion.21), channel_id=1, source_target_pairs={{0,1},{1,2},{2,3},{3,4},{4,5},{5,6},{6,7},{7,8},{8,9},{9,10},{10,1... | collective-permute-start | bytes 1179656 | tf_op jit(solution)/shard_map/ppermute | solution.py:19
  60.5 1.5 %collective-permute-start.3 = (bf16[2,2,2,64,384]{4,3,2,1,0:T(8,128)(2,1)S(1)}, bf16[2,2,2,64,384]{4,3,2,1,0:T(8,128)(2,1)S(1)}, u32[]{:S(2)}, u32[]{:S(2)}) collective-permute-start(bf16[2,2,2,64,384]{4,3,2,1,0:T(8,128)(2,1)S(1)} %fusion.21), channel_id=1, source_target_pairs={{1,0},{2,1},{3,2},{4,3},{5,4},{6,5},{7,6},{8,7},{9,8},{10,9},{11,1... | collective-permute-start | bytes 1179656 | tf_op jit(solution)/shard_map/ppermute | solution.py:22
  62.0 1.4 %maximum_convert_fusion = f32[6,2,2,64,384]{4,3,2,1,0:T(8,128)S(1)} fusion(bf16[2,2,2,64,384]{4,3,2,1,0:T(8,128)(2,1)} %collective-permute-done.5, bf16[2,2,2,64,384]{4,3,2,1,0:T(8,128)(2,1)} %convert_element_type.52, bf16[2,2,2,64,384]{4,3,2,1,0:T(8,128)(2,1)} %collective-permute-done.4), kind=kLoop, calls=%fused_computation.23 | loop fusion | flops 1769472 | bytes 3538944 | tf_op jit(solution)/shard_map/convert_element_type | solution.py:140
  63.7 1.5 %collective-permute-done.3 = bf16[2,2,2,64,384]{4,3,2,1,0:T(8,128)(2,1)S(1)} collective-permute-done((bf16[2,2,2,64,384]{4,3,2,1,0:T(8,128)(2,1)S(1)}, bf16[2,2,2,64,384]{4,3,2,1,0:T(8,128)(2,1)S(1)}, u32[]{:S(2)}, u32[]{:S(2)}) %collective-permute-start.3) | collective-permute-done | bytes 393248 | tf_op jit(solution)/shard_map/ppermute | solution.py:22
  71.7 2.0 %copy.48 = bf16[2,2,15,64,384]{4,3,2,1,0:T(8,128)(2,1)} copy(bf16[2,2,15,64,384]{4,3,1,0,2:T(8,128)(2,1)S(1)} %fusion.37) | data formatting | bytes 5898240 | tf_op jit(solution)/shard_map/stack | solution.py:43
  79.8 2.7 %reshape.120 = f32[2,16,2,64,64]{4,3,2,0,1:T(8,128)} reshape(f32[2,16,2,32,128]{4,3,2,0,1:T(8,128)} %all-to-all-done.1) | data formatting | bytes 2097152 | tf_op jit(solution)/shard_map/reshape | solution.py:110
  82.5 3.4 %fusion.10 = f32[2,8,64,64]{3,1,2,0:T(8,128)S(1)} fusion(f32[2,16,2,64,64]{4,3,2,0,1:T(8,128)} %reshape.120, s32[2,16,2]{1,2,0:T(2,128)S(1)} %copy.32), kind=kOutput, calls=%fused_computation.18 | convolution fusion | flops 25166336 | bytes 1310976 | tf_op jit(solution)/shard_map/pncr,pncqs->prqs/dot_general | solution.py:112
  86.8 1.9 %reshape.92 = f32[2,8,32,128]{3,2,1,0:T(8,128)} reshape(f32[2,8,64,64]{3,2,1,0:T(8,128)} %copy.37) | data formatting | bytes 524288 | tf_op jit(solution)/shard_map/reshape | solution.py:116
  88.7 1.8 %fusion.100 = (bf16[2,8,32,128]{3,2,1,0:T(8,128)(2,1)}, f32[2,8,32,128]{3,2,1,0:T(8,128)}) fusion(f32[2,8,32,128]{3,2,1,0:T(8,128)} %reshape.92, f32[2,8,32,128]{3,2,1,0:T(8,128)} %param.9), kind=kLoop, calls=%fused_computation.189 | loop fusion | flops 131072 | bytes 917504 | tf_op jit(solution)/shard_map/convert_element_type | solution.py:118
  90.5 1.7 %reshape.93 = bf16[2,8,64,64]{3,2,1,0:T(8,128)(2,1)} reshape(bf16[2,8,32,128]{3,2,1,0:T(8,128)(2,1)} %get-tuple-element.2) | data formatting | bytes 262144 | tf_op jit(solution)/shard_map/reshape | solution.py:119
  92.3 1.4 %convolution_convert_fusion = bf16[2,16,2,64,64]{4,1,3,2,0:T(8,128)(2,1)S(1)} fusion(bf16[2,8,64,64,1]{3,2,1,0,4:T(8,128)(2,1)} %bitcast.364, s32[2,16,2]{1,2,0:T(2,128)S(1)} %copy.32), kind=kOutput, calls=%fused_computation.17 | convolution fusion | flops 4457984 | bytes 655616 | tf_op jit(solution)/shard_map/pncr,prqs->pncqs/dot_general | solution.py:120
  93.7 1.3 copy.84
  95.0 3.0 %reshape.121 = bf16[16,2,8192]{2,1,0:T(2,128)(2,1)} reshape(bf16[16,2,2,64,64]{4,3,2,1,0:T(8,128)(2,1)} %bitcast.358) | data formatting | bytes 1048576
  98.0 18.3 %all-to-all-start.2 = ((bf16[16,2,8192]{2,1,0:T(2,128)(2,1)}), bf16[16,2,8192]{2,1,0:T(2,128)(2,1)}, u32[]{:S(2)}, u32[]{:S(2)}) async-start(bf16[16,2,8192]{2,1,0:T(2,128)(2,1)} %reshape.121), calls=%async_computation.2 | async-start | bytes 1048576 | tf_op jit(solution)/shard_map/all_to_all | solution.py:126
  117.8 2.4 %copy.51 = bf16[2,2,15,64,384]{4,3,2,1,0:T(8,128)(2,1)S(1)} copy(bf16[2,2,15,64,384]{4,3,1,0,2:T(8,128)(2,1)} %fusion.22) | data formatting | bytes 5898240 | tf_op jit(solution)/shard_map/stack | solution.py:43
  120.6 1.4 %convolution_bitcast_fusion.1 = f32[1,2,2,64,384]{4,3,2,1,0:T(8,128)} fusion(bf16[2,2,960,384]{3,2,1,0:T(8,128)(2,1)S(1)} %bitcast.353, bf16[64,960,1,1]{0,1,3,2:T(8,128)(2,1)S(1)} %bitcast.360), kind=kOutput, calls=%fused_computation.20 | convolution fusion | flops 188743680 | bytes 3465216 | tf_op jit(solution)/shard_map/ok,xykz->xyoz/dot_general | solution.py:46
  122.0 1.4 %convolution_bitcast_fusion = f32[1,2,2,64,384]{4,3,2,1,0:T(8,128)} fusion(bf16[2,2,960,384]{3,2,1,0:T(8,128)(2,1)S(1)} %bitcast.356, bf16[64,960,1,1]{0,1,3,2:T(8,128)(2,1)S(1)} %bitcast.361), kind=kOutput, calls=%fused_computation.19 | convolution fusion | flops 188743680 | bytes 3465216 | tf_op jit(solution)/shard_map/ok,xykz->xyoz/dot_general | solution.py:46
  123.4 7.4 %all-to-all-done.2 = bf16[16,2,8192]{2,1,0:T(2,128)(2,1)} async-done(((bf16[16,2,8192]{2,1,0:T(2,128)(2,1)}), bf16[16,2,8192]{2,1,0:T(2,128)(2,1)}, u32[]{:S(2)}, u32[]{:S(2)}) %all-to-all-start.2) | async-done | bytes 524320 | tf_op jit(solution)/shard_map/all_to_all | solution.py:126
  130.8 2.3 %reshape.122 = bf16[16,2,2,64,64]{4,3,2,1,0:T(8,128)(2,1)S(1)} reshape(bf16[16,2,8192]{2,1,0:T(2,128)(2,1)} %all-to-all-done.2) | data formatting | bytes 1048576
  134.3 2.6 %fusion.15 = f32[2,2,2,64,384]{4,3,2,1,0:T(8,128)} fusion(f32[4,2,2,64,384]{4,3,2,1,0:T(8,128)S(1)} %fusion.3, f32[2,2,2,64,384]{4,3,2,1,0:T(8,128)S(1)} %bitcast.359, f32[1,2,2,64,384]{4,3,2,1,0:T(8,128)} %convolution_bitcast_fusion, f32[1,2,2,64,384]{4,3,2,1,0:T(8,128)} %convolution_bitcast_fusion.1, f32[2,2,2,64,384]{4,3,2,1,0:T(8,128)S(1)} %copy-done.2, ...), kind=kLoop, calls=%fused_computation.29 | loop fusion | flops 1966080 | bytes 6291456 | tf_op jit(solution)/shard_map/add | solution.py:150
  (107 shorter events, 31.0 us)
Async XLA Ops:
  0.6 24.2 %copy-start = (bf16[2,1,64,384]{3,2,1,0:T(8,128)(2,1)S(1)}, bf16[2,1,64,384]{3,2,1,0:T(8,128)(2,1)}, u32[]{:S(2)}) copy-start(bf16[2,1,64,384]{3,2,1,0:T(8,128)(2,1)} %param.10) | copy-start | bytes 294916
  2.6 47.3 %collective-permute-start = (bf16[2,2,2,64,384]{4,3,2,1,0:T(8,128)(2,1)}, bf16[2,2,2,64,384]{4,3,2,1,0:T(8,128)(2,1)}, u32[]{:S(2)}, u32[]{:S(2)}) collective-permute-start(bf16[2,2,2,64,384]{4,3,2,1,0:T(8,128)(2,1)} %convert_element_type.52), channel_id=1, source_target_pairs={{0,1},{1,2},{2,3},{3,4},{4,5},{5,6},{6,7},{7,8},{8,9},{9,10},{10,1... | collective-permute-start | bytes 1179656 | tf_op jit(solution)/shard_map/ppermute | solution.py:19
  5.7 44.2 %collective-permute-start.1 = (bf16[2,2,2,64,384]{4,3,2,1,0:T(8,128)(2,1)}, bf16[2,2,2,64,384]{4,3,2,1,0:T(8,128)(2,1)}, u32[]{:S(2)}, u32[]{:S(2)}) collective-permute-start(bf16[2,2,2,64,384]{4,3,2,1,0:T(8,128)(2,1)} %convert_element_type.52), channel_id=1, source_target_pairs={{1,0},{2,1},{3,2},{4,3},{5,4},{6,5},{7,6},{8,7},{9,8},{10,9},{11,1... | collective-permute-start | bytes 1179656 | tf_op jit(solution)/shard_map/ppermute | solution.py:22
  7.0 54.9 %collective-permute-start.4 = (bf16[2,2,2,64,384]{4,3,2,1,0:T(8,128)(2,1)}, bf16[2,2,2,64,384]{4,3,2,1,0:T(8,128)(2,1)}, u32[]{:S(2)}, u32[]{:S(2)}) collective-permute-start(bf16[2,2,2,64,384]{4,3,2,1,0:T(8,128)(2,1)} %convert_element_type.52), channel_id=1, source_target_pairs={{0,16},{1,17},{2,18},{3,19},{4,20},{5,21},{6,22},{7,23},{8,24},{9,... | collective-permute-start | bytes 1179656 | tf_op jit(solution)/shard_map/ppermute | solution.py:19
  12.0 50.0 %collective-permute-start.5 = (bf16[2,2,2,64,384]{4,3,2,1,0:T(8,128)(2,1)}, bf16[2,2,2,64,384]{4,3,2,1,0:T(8,128)(2,1)}, u32[]{:S(2)}, u32[]{:S(2)}) collective-permute-start(bf16[2,2,2,64,384]{4,3,2,1,0:T(8,128)(2,1)} %convert_element_type.52), channel_id=1, source_target_pairs={{16,0},{17,1},{18,2},{19,3},{20,4},{21,5},{22,6},{23,7},{24,8},{25... | collective-permute-start | bytes 1179656 | tf_op jit(solution)/shard_map/ppermute | solution.py:22
  14.7 29.1 %all-to-all-start = ((s32[2,16,2]{2,0,1:T(2,128)}), s32[2,16,2]{2,0,1:T(2,128)S(1)}, u32[]{:S(2)}, u32[]{:S(2)}) async-start(s32[2,16,2]{2,0,1:T(2,128)} %copy.31), calls=%async_computation | async-start | bytes 32768 | tf_op jit(solution)/shard_map/all_to_all | solution.py:108
  43.8 36.0 %all-to-all-start.1 = ((f32[2,16,2,32,128]{4,3,2,0,1:T(8,128)}), f32[2,16,2,32,128]{4,3,2,0,1:T(8,128)}, u32[]{:S(2)}, u32[]{:S(2)}) async-start(f32[2,16,2,32,128]{4,3,2,0,1:T(8,128)} %copy_multiply_fusion), calls=%async_computation.1 | async-start | bytes 2097152 | tf_op jit(solution)/shard_map/all_to_all | solution.py:107
  55.7 0.9 copy-start.5
  56.7 1.4 %copy-start.2 = (f32[2,2,2,64,384]{4,3,2,1,0:T(8,128)S(1)}, f32[2,2,2,64,384]{4,3,2,1,0:T(8,128)}, u32[]{:S(2)}) copy-start(f32[2,2,2,64,384]{4,3,2,1,0:T(8,128)} %param.8) | copy-start | bytes 2359300
  57.4 4.6 %copy-start.3 = (f32[1,2,2,64,384]{4,3,2,1,0:T(8,128)}, f32[1,2,2,64,384]{4,3,2,1,0:T(8,128)S(1)}, u32[]{:S(2)}) copy-start(f32[1,2,2,64,384]{4,3,2,1,0:T(8,128)S(1)} %convolution_bitcast_fusion.3) | copy-start | bytes 1179652
  58.1 3.9 %copy-start.4 = (f32[1,2,2,64,384]{4,3,2,1,0:T(8,128)}, f32[1,2,2,64,384]{4,3,2,1,0:T(8,128)S(1)}, u32[]{:S(2)}) copy-start(f32[1,2,2,64,384]{4,3,2,1,0:T(8,128)S(1)} %convolution_bitcast_fusion.2) | copy-start | bytes 1179652
  58.2 5.5 %collective-permute-start.2 = (bf16[2,2,2,64,384]{4,3,2,1,0:T(8,128)(2,1)S(1)}, bf16[2,2,2,64,384]{4,3,2,1,0:T(8,128)(2,1)S(1)}, u32[]{:S(2)}, u32[]{:S(2)}) collective-permute-start(bf16[2,2,2,64,384]{4,3,2,1,0:T(8,128)(2,1)S(1)} %fusion.21), channel_id=1, source_target_pairs={{0,1},{1,2},{2,3},{3,4},{4,5},{5,6},{6,7},{7,8},{8,9},{9,10},{10,1... | collective-permute-start | bytes 1179656 | tf_op jit(solution)/shard_map/ppermute | solution.py:19
  60.5 4.7 %collective-permute-start.3 = (bf16[2,2,2,64,384]{4,3,2,1,0:T(8,128)(2,1)S(1)}, bf16[2,2,2,64,384]{4,3,2,1,0:T(8,128)(2,1)S(1)}, u32[]{:S(2)}, u32[]{:S(2)}) collective-permute-start(bf16[2,2,2,64,384]{4,3,2,1,0:T(8,128)(2,1)S(1)} %fusion.21), channel_id=1, source_target_pairs={{1,0},{2,1},{3,2},{4,3},{5,4},{6,5},{7,6},{8,7},{9,8},{10,9},{11,1... | collective-permute-start | bytes 1179656 | tf_op jit(solution)/shard_map/ppermute | solution.py:22
  98.0 32.9 %all-to-all-start.2 = ((bf16[16,2,8192]{2,1,0:T(2,128)(2,1)}), bf16[16,2,8192]{2,1,0:T(2,128)(2,1)}, u32[]{:S(2)}, u32[]{:S(2)}) async-start(bf16[16,2,8192]{2,1,0:T(2,128)(2,1)} %reshape.121), calls=%async_computation.2 | async-start | bytes 1048576 | tf_op jit(solution)/shard_map/all_to_all | solution.py:126
  117.8 2.7 %copy-start.1 = (bf16[2,2,15,64,384]{4,3,2,1,0:T(8,128)(2,1)S(1)}, bf16[2,2,15,64,384]{4,3,2,1,0:T(8,128)(2,1)}, u32[]{:S(2)}) copy-start(bf16[2,2,15,64,384]{4,3,2,1,0:T(8,128)(2,1)} %copy.48) | copy-start | bytes 8847364
  122.0 11.1 %copy-start.6 = (s32[2,1,16,2]{2,3,1,0:T(2,128)S(1)}, s32[2,1,16,2]{2,3,1,0:T(2,128)}, u32[]{:S(2)}) copy-start(s32[2,1,16,2]{2,3,1,0:T(2,128)} %param.13) | copy-start | bytes 772
where the time goes:
time: 139 us; the launch traced here: 137 us
  local copies, waits for them, and re-layouts  52.6 us (38%)
  starting transfers between devices  46.5 us (33%)
  other arithmetic  16.1 us (12%)
  matrix products  11.5 us (8%)
  waiting for transfers between devices  8.91 us (6%)
    unnamed x72, local copies, waits for them, and re-layouts  21.1 us
    all_to_all x1, starting transfers between devices, on_device(): lax.all_to_all(rows_back, 'tiles', split_axis=1, concat_axis=1, tiled=True)  18.3 us
    ppermute x3, starting transfers between devices, extended_2(): lax.ppermute(lax.slice_in_dim(block, block.shape[dim] - width, None, axis...  10.4 us
    all_to_all x1, starting transfers between devices, on_device(): lax.all_to_all(readout_pick, 'tiles', split_axis=1, concat_axis=1, tiled=...  7.71 us
    all_to_all x1, waiting for transfers between devices, on_device(): lax.all_to_all(rows_back, 'tiles', split_axis=1, concat_axis=1, tiled=True)  7.41 us
    another operation x1, local copies, waits for them, and re-layouts, real_form(): blocks = jnp.stack([upper_half, lower_half], axis=-3)  6.86 us
    another operation x7, local copies, waits for them, and re-layouts, stencil(): stacked = jnp.stack(shifted, axis=2)  6.09 us
    all_to_all x1, starting transfers between devices, on_device(): lax.all_to_all(partial_value, 'tiles', split_axis=1, concat_axis=1, tiled...  6.07 us
  transfers between devices with their start and end apart: 9, of which 2 were waited for; matrix products, arithmetic and copies ran while one was open for 39% of the time, Pallas kernels for 0%

commit v1 on v0

v1 whole, which is shorter than its diff:
```python
import functools

import jax
import jax.numpy as jnp
from jax import lax
from jax.experimental import pallas as pl
from jax.experimental.pallas import tpu as pltpu
from jax.sharding import PartitionSpec as P

SPIRIT_WEIGHT = 1.0
PHASE_WEIGHT = 0.15

BF = jnp.bfloat16
F32 = jnp.float32


def dot(a, b):
    return jnp.dot(a, b, preferred_element_type=F32)


def dot_t(a, b):
    return lax.dot_general(a, b, (((1,), (1,)), ((), ())), preferred_element_type=F32)


def onehot(mask):
    return jnp.where(mask, 1.0, 0.0).astype(BF)


def iota(shape, dim):
    return lax.broadcasted_iota(jnp.int32, shape, dim)


def build_matrix(taps_ref, out_ref, coils, kx, kz, planes, adjoint):
    taps = taps_ref[...]
    half = kx * coils
    chan = 2 * coils
    width = (planes + kx - 1) * chan
    src = iota((half, width), 0)
    col = iota((half, width), 1)
    rows = iota((chan, chan), 0)
    cols = iota((chan, chan), 1)
    weave = onehot(rows == jnp.where(cols < coils, 2 * cols, 2 * (cols - coils) + 1))
    tap_a = src // coils
    coil = src % coils
    for x in range(planes):
        plane = (x + kx - 1 - tap_a) if adjoint else (x + tap_a)
        base = plane * chan + 2 * coil
        even = jnp.where(col == base, 1.0, 0.0)
        odd = jnp.where(col == base + 1, 1.0, 0.0)
        sign = -1.0 if not adjoint else 1.0
        first = jnp.concatenate([even, sign * odd], axis=0).astype(BF)
        second = jnp.concatenate([odd, -sign * even], axis=0).astype(BF)
        upper = dot(taps, first).astype(BF)
        lower = dot(taps, second).astype(BF)
        for c in range(kz):
            both = jnp.concatenate(
                [upper[c * coils : (c + 1) * coils], lower[c * coils : (c + 1) * coils]], axis=0
            )
            row = (c * planes + x) * chan
            out_ref[row : row + chan, :] = dot(weave, both).astype(BF)


def stencil(weights, window, rows, up):
    prod = dot(weights, window)
    depth = prod.shape[1]
    lane = iota((rows, depth), 1)
    first, mid, last = prod[:rows], prod[rows : 2 * rows], prod[2 * rows : 3 * rows]
    if up:
        first, last = last, first
    first = jnp.where(lane == 0, 0.0, pltpu.roll(first, 1, 1))
    last = jnp.where(lane == depth - 1, 0.0, pltpu.roll(last, depth - 1, 1))
    return first + mid + last


def kernel(
    dims,
    meta,
    grid,
    samples,
    interp,
    fwd_taps,
    adj_taps,
    grad,
    resid,
    ext,
    ext2,
    plo,
    phi,
    image,
    snd,
    rcv,
    back_snd,
    back_rcv,
    racc,
    lacc,
    w_fwd,
    w_adj,
    halo_send,
    halo_recv,
    ph_send,
    ph_recv,
    a_send,
    a_recv,
    b_send,
    b_recv,
):
    slabs, tiles, phases, planes, rows_y, chan, depth, kx, kz, cap, reads = dims
    coils = chan // 2
    lines = planes * rows_y
    own = planes * chan
    slots = phases * cap
    seg = interp.shape[2]
    slab = lax.axis_index("phases")
    me = lax.axis_index("tiles")

    barrier = pltpu.get_barrier_semaphore()

    @pl.loop(1, tiles)
    def _(k):
        pl.semaphore_signal(barrier, inc=1, device_id={"tiles": lax.rem(me + k, tiles)})

    @pl.when(slab > 0)
    def _():
        pl.semaphore_signal(barrier, inc=1, device_id={"phases": slab - 1})

    @pl.when(slab < slabs - 1)
    def _():
        pl.semaphore_signal(barrier, inc=1, device_id={"phases": slab + 1})

    for p in range(phases):
        for x in range(planes):
            for y in range(rows_y):
                ext[p, y, own + x * chan : own + (x + 1) * chan, :] = grid[p, x, y].astype(BF)

    def zero_edges(ref):
        @pl.when(me == 0)
        def _():
            ref[:, :, :own, :] = jnp.zeros((phases, rows_y, own, depth), BF)

        @pl.when(me == tiles - 1)
        def _():
            ref[:, :, 2 * own :, :] = jnp.zeros((phases, rows_y, own, depth), BF)

    zero_edges(ext)
    zero_edges(ext2)

    @pl.when(slab == 0)
    def _():
        plo[...] = jnp.zeros(plo.shape, BF)

    @pl.when(slab == slabs - 1)
    def _():
        phi[...] = jnp.zeros(phi.shape, BF)

    rows_i = iota((chan, chan), 0)
    cols_i = iota((chan, chan), 1)
    split = onehot(cols_i == jnp.where(rows_i < coils, 2 * rows_i, 2 * (rows_i - coils) + 1))
    weave = onehot(rows_i == jnp.where(cols_i < coils, 2 * cols_i, 2 * (cols_i - coils) + 1))
    zero_w = jnp.zeros((seg, depth), BF)
    for p in range(phases):
        w = interp[p, 0]
        w_even = jnp.concatenate([w, zero_w], axis=0)
        w_odd = jnp.concatenate([zero_w, w], axis=0)
        for l in range(lines):
            x, y = l // rows_y, l % rows_y
            parted = dot(split, ext[p, y, own + x * chan : own + (x + 1) * chan, :]).astype(BF)
            image[p * lines + l] = dot_t(parted[:coils], w_even) + dot_t(parted[coils:], w_odd)

    peers = tiles - 1 + jnp.where(slab > 0, 1, 0) + jnp.where(slab < slabs - 1, 1, 0)
    pl.semaphore_wait(barrier, peers)

    def halo(ref, index, right):
        if right:
            src, dst, target = (own, 2 * own), (0, own), me + 1
        else:
            src, dst, target = (own, 2 * own), (2 * own, 3 * own), me - 1
        return pltpu.make_async_remote_copy(
            src_ref=ref.at[:, :, src[0] : src[1], :],
            dst_ref=ref.at[:, :, dst[0] : dst[1], :],
            send_sem=halo_send.at[index],
            recv_sem=halo_recv.at[index],
            device_id={"tiles": target},
        )

    def start_halo(ref, index):
        @pl.when(me < tiles - 1)
        def _():
            halo(ref, index, True).start()

        @pl.when(me > 0)
        def _():
            halo(ref, index + 1, False).start()

    def wait_halo(ref, index):
        @pl.when(me > 0)
        def _():
            halo(ref, index, True).wait_recv()

        @pl.when(me < tiles - 1)
        def _():
            halo(ref, index + 1, False).wait_recv()

    def end_halo(ref, index):
        @pl.when(me < tiles - 1)
        def _():
            halo(ref, index, True).wait_send()

        @pl.when(me > 0)
        def _():
            halo(ref, index + 1, False).wait_send()

    def phase_copy(up):
        return pltpu.make_async_remote_copy(
            src_ref=ext.at[:, :, own : 2 * own, :],
            dst_ref=plo if up else phi,
            send_sem=ph_send.at[0 if up else 1],
            recv_sem=ph_recv.at[0 if up else 1],
            device_id={"phases": slab + 1 if up else slab - 1},
        )

    start_halo(ext, 0)

    def line_of(p, o, c):
        return meta[p, o * cap + c]

    def read_of(p, o, c):
        return meta[p, (tiles + o) * cap + c]

    def live_of(p, o, c):
        return jnp.where(c < meta[p, 2 * tiles * cap + o], 1.0, 0.0)

    pad = snd.shape[1] - slots * coils

    def fill(o, ref):
        ids = jnp.zeros((pad, 2 * seg), F32)
        row = iota((pad, 2 * seg), 0)
        for p in range(phases):
            for c in range(cap):
                s = p * cap + c
                value = image[p * lines + line_of(p, o, c)] * live_of(p, o, c)
                ref[o, s * coils : (s + 1) * coils, :] = value.astype(BF)
                ids = jnp.where(row == s, read_of(p, o, c).astype(F32), ids)
        ref[o, slots * coils :, :] = ids.astype(BF)

    def there(o):
        return pltpu.make_async_remote_copy(
            src_ref=snd.at[o],
            dst_ref=rcv.at[me],
            send_sem=a_send.at[o],
            recv_sem=a_recv.at[me],
            device_id={"tiles": o},
        )

    def arrived(t):
        return pltpu.make_async_remote_copy(
            src_ref=snd.at[t],
            dst_ref=rcv.at[t],
            send_sem=a_send.at[t],
            recv_sem=a_recv.at[t],
            device_id={"tiles": t},
        )

    def back(t):
        return pltpu.make_async_remote_copy(
            src_ref=back_snd.at[t],
            dst_ref=back_rcv.at[me],
            send_sem=b_send.at[t],
            recv_sem=b_recv.at[me],
            device_id={"tiles": t},
        )

    def returned(o):
        return pltpu.make_async_remote_copy(
            src_ref=back_snd.at[o],
            dst_ref=back_rcv.at[o],
            send_sem=b_send.at[o],
            recv_sem=b_recv.at[o],
            device_id={"tiles": o},
        )

    @pl.loop(1, tiles)
    def _(k):
        o = lax.rem(me + k, tiles)
        fill(o, snd)
        there(o).start()

    fill(me, rcv)

    @pl.when(slab < slabs - 1)
    def _():
        phase_copy(True).start()

    @pl.when(slab > 0)
    def _():
        phase_copy(False).start()

    build_matrix(fwd_taps, w_fwd, coils, kx, kz, planes, False)
    build_matrix(adj_taps, w_adj, coils, kx, kz, planes, True)

    wait_halo(ext, 0)
    for p in range(phases):
        for y in range(rows_y):
            out = stencil(w_fwd[...], ext[p, y], own, False)
            for x in range(planes):
                rest = out[x * chan : (x + 1) * chan] - grid[p, x, y]
                grad[p, x, y] = -SPIRIT_WEIGHT * rest
                ext2[p, y, own + x * chan : own + (x + 1) * chan, :] = rest.astype(BF)
    start_halo(ext2, 2)

    for p in range(phases):
        for r in range(reads):
            racc[p, r] = -samples[p, r]

    def add_from(t):
        ids = rcv[t, slots * coils :, :].astype(F32)
        for p in range(phases):
            for c in range(cap):
                s = p * cap + c
                value = rcv[t, s * coils : (s + 1) * coils, :].astype(F32)
                own_id = jnp.broadcast_to(ids[s : s + 1], value.shape)
                for r in range(reads):
                    racc[p, r] = racc[p, r] + jnp.where(own_id == r, value, 0.0)

    add_from(me)

    @pl.loop(1, tiles)
    def _(k):
        t = lax.rem(me + tiles - k, tiles)
        arrived(t).wait_recv()
        add_from(t)

    for p in range(phases):
        for r in range(reads):
            value = racc[p, r]
            resid[p, r] = value
            racc[p, r] = value.astype(BF).astype(F32)

    def pick_for(t, ref):
        ids = rcv[t, slots * coils :, :].astype(F32)
        for p in range(phases):
            for c in range(cap):
                s = p * cap + c
                own_id = jnp.broadcast_to(ids[s : s + 1], (coils, 2 * seg))
                value = jnp.zeros((coils, 2 * seg), F32)
                for r in range(reads):
                    value = jnp.where(own_id == r, racc[p, r], value)
                ref[t, s * coils : (s + 1) * coils, :] = value.astype(BF)

    @pl.loop(1, tiles)
    def _(k):
        t = lax.rem(me + k, tiles)
        pick_for(t, back_snd)
        back(t).start()

    pick_for(me, back_rcv)

    @pl.when(slab > 0)
    def _():
        phase_copy(True).wait_recv()

    @pl.when(slab < slabs - 1)
    def _():
        phase_copy(False).wait_recv()

    below = jnp.where(slab > 0, 1.0, 0.0)
    above = jnp.where(slab < slabs - 1, 1.0, 0.0)
    for y in range(rows_y):
        for x in range(planes):
            part = slice(x * chan, (x + 1) * chan)
            field = [plo[phases - 2, y, part, :].astype(F32), plo[phases - 1, y, part, :].astype(F32)]
            field += [grid[p, x, y] for p in range(phases)]
            field += [phi[0, y, part, :].astype(F32), phi[1, y, part, :].astype(F32)]
            diff = [field[i] - 2.0 * field[i + 1] + field[i + 2] for i in range(phases + 2)]
            diff[0] = diff[0] * below
            diff[-1] = diff[-1] * above
            for p in range(phases):
                bend = diff[p] - 2.0 * diff[p + 1] + diff[p + 2]
                grad[p, x, y] = grad[p, x, y] + PHASE_WEIGHT * bend

    wait_halo(ext2, 2)
    for p in range(phases):
        for y in range(rows_y):
            out = stencil(w_adj[...], ext2[p, y], own, True)
            for x in range(planes):
                part = out[x * chan : (x + 1) * chan]
                grad[p, x, y] = grad[p, x, y] + SPIRIT_WEIGHT * part

    for i in range(phases * lines):
        lacc[i] = jnp.zeros((coils, 2 * seg), F32)

    def spread_from(o):
        for p in range(phases):
            for c in range(cap):
                s = p * cap + c
                value = back_rcv[o, s * coils : (s + 1) * coils, :].astype(F32) * live_of(p, o, c)
                line = line_of(p, o, c)
                for l in range(lines):
                    weight = jnp.where(line == l, 1.0, 0.0)
                    lacc[p * lines + l] = lacc[p * lines + l] + value * weight

    spread_from(me)

    @pl.loop(1, tiles)
    def _(k):
        o = lax.rem(me + tiles - k, tiles)
        returned(o).wait_recv()
        spread_from(o)

    lane = iota((coils, 2 * seg), 1)
    for p in range(phases):
        w = interp[p, 0]
        four = jnp.concatenate([w, w, w, w], axis=0)
        for l in range(lines):
            x, y = l // rows_y, l % rows_y
            total = lacc[p * lines + l]
            high = total.astype(BF).astype(F32)
            rest = total - high
            even = [jnp.where(lane < seg, v, 0.0) for v in (high, rest)]
            odd = [jnp.where(lane < seg, 0.0, v) for v in (high, rest)]
            both = jnp.concatenate(
                [jnp.concatenate(even, axis=1), jnp.concatenate(odd, axis=1)], axis=0
            ).astype(BF)
            woven = dot(weave, both).astype(BF)
            grad[p, x, y] = grad[p, x, y] + dot(woven, four)

    end_halo(ext, 0)
    end_halo(ext2, 2)

    @pl.when(slab < slabs - 1)
    def _():
        phase_copy(True).wait_send()

    @pl.when(slab > 0)
    def _():
        phase_copy(False).wait_send()

    @pl.loop(1, tiles)
    def _(k):
        o = lax.rem(me + k, tiles)
        there(o).wait_send()
        back(o).wait_send()


def on_device(
    slabs,
    tiles,
    kspace_grid,
    samples,
    interp_matrix,
    kernel_real,
    kernel_imag,
    segment_line,
    segment_readout,
    segment_count,
):
    phases, planes, rows_y, chan, depth = kspace_grid.shape
    kx, kz, coils, _ = kernel_real.shape
    cap = segment_line.shape[3]
    reads = samples.shape[1]
    seg = interp_matrix.shape[2]
    own = planes * chan
    slots = phases * cap
    message = slots * coils + 16 * -(-slots // 16)
    lines = planes * rows_y
    width = (planes + kx - 1) * chan
    meta = jnp.concatenate(
        [
            segment_line.reshape(phases, -1),
            segment_readout.reshape(phases, -1),
            segment_count.reshape(phases, -1),
        ],
        axis=1,
    )
    both = jnp.stack([kernel_real, kernel_imag])
    fwd_taps = jnp.transpose(both, (2, 3, 0, 1, 4)).reshape(kz * coils, 2 * kx * coils)
    adj_taps = jnp.transpose(both, (2, 4, 0, 1, 3)).reshape(kz * coils, 2 * kx * coils)
    dims = (slabs, tiles, phases, planes, rows_y, chan, depth, kx, kz, cap, reads)
    vmem = pl.BlockSpec(memory_space=pltpu.VMEM)
    dma = pltpu.SemaphoreType.DMA
    return pl.pallas_call(
        functools.partial(kernel, dims),
        out_shape=(
            jax.ShapeDtypeStruct(kspace_grid.shape, F32),
            jax.ShapeDtypeStruct(samples.shape, F32),
        ),
        in_specs=[pl.BlockSpec(memory_space=pltpu.SMEM)] + [vmem] * 5,
        out_specs=(vmem, vmem),
        scratch_shapes=[
            pltpu.VMEM((phases, rows_y, 3 * own, depth), BF),
            pltpu.VMEM((phases, rows_y, 3 * own, depth), BF),
            pltpu.VMEM((phases, rows_y, own, depth), BF),
            pltpu.VMEM((phases, rows_y, own, depth), BF),
            pltpu.VMEM((phases * lines, coils, 2 * seg), F32),
            pltpu.VMEM((tiles, message, 2 * seg), BF),
            pltpu.VMEM((tiles, message, 2 * seg), BF),
            pltpu.VMEM((tiles, slots * coils, 2 * seg), BF),
            pltpu.VMEM((tiles, slots * coils, 2 * seg), BF),
            pltpu.VMEM((phases, reads, coils, 2 * seg), F32),
            pltpu.VMEM((phases * lines, coils, 2 * seg), F32),
            pltpu.VMEM((kz * own, width), BF),
            pltpu.VMEM((kz * own, width), BF),
            dma((4,)),
            dma((4,)),
            dma((2,)),
            dma((2,)),
            dma((tiles,)),
            dma((tiles,)),
            dma((tiles,)),
            dma((tiles,)),
        ],
        compiler_params=pltpu.CompilerParams(
            collective_id=0, has_side_effects=True, vmem_limit_bytes=48 * 1024 * 1024
        ),
    )(meta, kspace_grid, samples, interp_matrix, fwd_taps, adj_taps)


def solution(mesh):
    return jax.shard_map(
        functools.partial(on_device, mesh.shape["phases"], mesh.shape["tiles"]),
        mesh=mesh,
        in_specs=(
            P("phases", "tiles", None, None, None),
            P("phases", "tiles", None, None),
            P("phases", "tiles", None, None),
            P(),
            P(),
            P("phases", "tiles", None, None),
            P("phases", "tiles", None, None),
            P("phases", "tiles", None),
        ),
        out_specs=(P("phases", "tiles", None, None, None), P("phases", "tiles", None, None)),
        check_vma=False,
    )
```

time: 139 us -> 48.3 us (0.35); the launches traced: 137 us -> 48 us
  local copies, waits for them, and re-layouts: 52.6 us -> 5.54 us
  starting transfers between devices: 46.5 us -> 0 us
  Pallas kernels: 0 us -> 40.7 us
  other arithmetic: 16.1 us -> 1.09 us
  matrix products: 11.5 us -> 0 us
  waiting for transfers between devices: 8.91 us -> 0 us
    pallas_call x0 -> x1, Pallas kernels: none -> 40.7 us  [on_device(): pl.pallas_call(functools.partial(kernel, dims), out_shape=(jax.ShapeDtype...]
    all_to_all x3 -> x0, starting transfers between devices: 32.1 us -> none  [the longest x1 18.3 us: on_device(): lax.all_to_all(rows_back, 'tiles', split_axis=1, concat_axis=1, tiled=True)]
    unnamed x72 -> x16, local copies, waits for them, and re-layouts: 21.1 us -> 4.38 us
    ppermute x6 -> x0, starting transfers between devices: 14.4 us -> none  [the longest x3 10.4 us: extended_2(): lax.ppermute(lax.slice_in_dim(block, block.shape[dim] - width, None, axis...]
    another operation x8 -> x0, local copies, waits for them, and re-layouts: 12.9 us -> none  [the longest x1 6.86 us: real_form(): blocks = jnp.stack([upper_half, lower_half], axis=-3)]
    dot_general x9 -> x0, matrix products: 11.5 us -> none  [the longest x4 4.19 us: stencil(): jnp.einsum('ok,xykz->xyoz', matrix, stacked, preferred_element_type=jnp.f...]
    all_to_all x3 -> x0, waiting for transfers between devices: 7.42 us -> none  [the longest x1 7.41 us: on_device(): lax.all_to_all(rows_back, 'tiles', split_axis=1, concat_axis=1, tiled=True)]
    transpose x2 -> x0, local copies, waits for them, and re-layouts: 6.12 us -> none  [the longest x1 4.24 us: on_device(): forward_matrix = jnp.transpose(blocks, (2, 0, 1, 3)).reshape(channels, -1)]
  transfers between devices with their start and end apart: 9 -> 0, of which waited for: 2 -> 0; matrix products, arithmetic and copies ran while one was open for 39% -> 0% of each run, Pallas kernels for 0% -> 0%
where the time goes in v1:
time: 48.3 us; the launch traced here: 48 us
  Pallas kernels  40.7 us (84%)
  local copies, waits for them, and re-layouts  5.54 us (11%)
  other arithmetic  1.09 us (2%)
  between operations  0.7 us (1%)
    pallas_call x1, Pallas kernels, on_device(): pl.pallas_call(functools.partial(kernel, dims), out_shape=(jax.ShapeDtype...  40.7 us
    unnamed x16, local copies, waits for them, and re-layouts  4.38 us
    transpose x1, other arithmetic, on_device(): jnp.transpose(both, (2, 4, 0, 1, 3)).reshape(kz * coils, 2 * kx * coils)  1.01 us

profile of v1, /device:TPU:0, one launch (start us, length us, event | category | flops | bytes accessed | tf_op | source)
XLA Modules:
  0.0 48.0 jit_solution(2873830245836723670)
XLA Ops:
  0.6 0.0 copy-start.3
  0.6 0.7 %copy-done.3 = s32[2,1,16,2]{2,3,1,0:T(2,128)S(1)} copy-done((s32[2,1,16,2]{2,3,1,0:T(2,128)S(1)}, s32[2,1,16,2]{2,3,1,0:T(2,128)}, u32[]{:S(2)}) %copy-start.3) | copy-done | bytes 280
  1.3 0.1 copy.14
  1.4 0.0 copy-start.4
  1.4 0.1 reshape.19
  1.5 0.6 %copy-done.4 = s32[2,1,16,2]{2,3,1,0:T(2,128)S(1)} copy-done((s32[2,1,16,2]{2,3,1,0:T(2,128)S(1)}, s32[2,1,16,2]{2,3,1,0:T(2,128)}, u32[]{:S(2)}) %copy-start.4) | copy-done | bytes 280
  2.1 0.1 copy.15
  2.2 0.0 copy-start.5
  2.2 0.1 reshape.20
  2.3 0.6 %copy-done.5 = s32[2,1,16]{2,1,0:T(1,128)S(1)} copy-done((s32[2,1,16]{2,1,0:T(1,128)S(1)}, s32[2,1,16]{2,1,0:T(1,128)}, u32[]{:S(2)}) %copy-start.5) | copy-done | bytes 152
  2.9 0.1 pad_add_fusion.meta
  2.9 1.0 %fusion = (bf16[3,32,2,5,32]{1,4,0,3,2:T(8,128)(2,1)S(1)}, bf16[3,32,2,5,32]{4,1,0,3,2:T(8,128)(2,1)S(1)}) fusion(bf16[1,5,3,32,32]{4,3,2,1,0:T(8,128)(2,1)} %bitcast.15, bf16[1,5,3,32,32]{4,3,2,1,0:T(8,128)(2,1)} %bitcast.16), kind=kLoop, calls=%fused_computation.1 | loop fusion | flops 30720 | bytes 184320 | tf_op jit(solution)/shard_map/transpose | solution.py:476
  3.9 0.3 copy.21
  4.3 0.0 copy-start
  4.3 0.2 reshape.25.adj_taps
  4.6 0.1 copy.20
  4.7 0.0 copy-start.1
  4.7 0.0 copy-start.2
  4.7 0.3 reshape.24.fwd_taps
  5.0 0.5 copy-done
  5.4 0.3 copy-done.1
  5.7 0.0 copy-done.2
  5.7 40.7 %shard_map.95 = (f32[2,2,2,64,384]{4,3,2,1,0:T(8,128)S(1)}, f32[2,8,32,128]{3,2,1,0:T(8,128)S(1)}) custom-call(s32[2,80]{1,0:T(2,128)S(1)} %pad_add_fusion.meta, f32[2,2,2,64,384]{4,3,2,1,0:T(8,128)S(1)} %copy-done, f32[2,8,32,128]{3,2,1,0:T(8,128)S(1)} %copy-done.1, bf16[2,1,64,384]{3,2,1,0:T(8,128)(2,1)S(1)} %copy-done.2, ...), custom_call_target="tpu_custom_call" | custom-call | tf_op jit(solution)/shard_map/pallas_call | solution.py:480
  46.4 0.9 %copy.26 = f32[2,2,2,64,384]{4,3,2,1,0:T(8,128)} copy(f32[2,2,2,64,384]{4,3,2,1,0:T(8,128)S(1)} %get-tuple-element.6) | data formatting | bytes 1572864
  47.3 0.7 %copy.27 = f32[2,8,32,128]{3,2,1,0:T(8,128)} copy(f32[2,8,32,128]{3,2,1,0:T(8,128)S(1)} %get-tuple-element.7) | data formatting | bytes 524288
Async XLA Ops:
  0.6 0.7 %copy-start.3 = (s32[2,1,16,2]{2,3,1,0:T(2,128)S(1)}, s32[2,1,16,2]{2,3,1,0:T(2,128)}, u32[]{:S(2)}) copy-start(s32[2,1,16,2]{2,3,1,0:T(2,128)} %param.13) | copy-start | bytes 772
  1.4 0.7 %copy-start.4 = (s32[2,1,16,2]{2,3,1,0:T(2,128)S(1)}, s32[2,1,16,2]{2,3,1,0:T(2,128)}, u32[]{:S(2)}) copy-start(s32[2,1,16,2]{2,3,1,0:T(2,128)} %param.14) | copy-start | bytes 772
  2.2 0.7 %copy-start.5 = (s32[2,1,16]{2,1,0:T(1,128)S(1)}, s32[2,1,16]{2,1,0:T(1,128)}, u32[]{:S(2)}) copy-start(s32[2,1,16]{2,1,0:T(1,128)} %param.15) | copy-start | bytes 388
  4.3 1.1 %copy-start = (f32[2,2,2,64,384]{4,3,2,1,0:T(8,128)S(1)}, f32[2,2,2,64,384]{4,3,2,1,0:T(8,128)}, u32[]{:S(2)}) copy-start(f32[2,2,2,64,384]{4,3,2,1,0:T(8,128)} %grid.1) | copy-start | bytes 2359300
  4.7 1.0 %copy-start.1 = (f32[2,8,32,128]{3,2,1,0:T(8,128)S(1)}, f32[2,8,32,128]{3,2,1,0:T(8,128)}, u32[]{:S(2)}) copy-start(f32[2,8,32,128]{3,2,1,0:T(8,128)} %samples.1) | copy-start | bytes 786436
  4.7 1.0 %copy-start.2 = (bf16[2,1,64,384]{3,2,1,0:T(8,128)(2,1)S(1)}, bf16[2,1,64,384]{3,2,1,0:T(8,128)(2,1)}, u32[]{:S(2)}) copy-start(bf16[2,1,64,384]{3,2,1,0:T(8,128)(2,1)} %interp.1) | copy-start | bytes 294916

commit v2 on v1

--- a/solution.py
+++ b/solution.py
@@ -30,34 +30,44 @@
     return lax.broadcasted_iota(jnp.int32, shape, dim)
 
 
-def build_matrix(taps_ref, out_ref, coils, kx, kz, planes, adjoint):
-    taps = taps_ref[...]
-    half = kx * coils
+def build_matrices(real_ref, imag_ref, fwd_ref, adj_ref, planes):
+    kx, kz, coils, _ = real_ref.shape
     chan = 2 * coils
-    width = (planes + kx - 1) * chan
-    src = iota((half, width), 0)
-    col = iota((half, width), 1)
+    real = real_ref[...].reshape(kx * kz * coils, coils)
+    imag = imag_ref[...].reshape(kx * kz * coils, coils)
+    src = iota((coils, 2 * chan), 0)
+    col = iota((coils, 2 * chan), 1)
     rows = iota((chan, chan), 0)
     cols = iota((chan, chan), 1)
     weave = onehot(rows == jnp.where(cols < coils, 2 * cols, 2 * (cols - coils) + 1))
-    tap_a = src // coils
-    coil = src % coils
-    for x in range(planes):
-        plane = (x + kx - 1 - tap_a) if adjoint else (x + tap_a)
-        base = plane * chan + 2 * coil
-        even = jnp.where(col == base, 1.0, 0.0)
-        odd = jnp.where(col == base + 1, 1.0, 0.0)
-        sign = -1.0 if not adjoint else 1.0
-        first = jnp.concatenate([even, sign * odd], axis=0).astype(BF)
-        second = jnp.concatenate([odd, -sign * even], axis=0).astype(BF)
-        upper = dot(taps, first).astype(BF)
-        lower = dot(taps, second).astype(BF)
-        for c in range(kz):
-            both = jnp.concatenate(
-                [upper[c * coils : (c + 1) * coils], lower[c * coils : (c + 1) * coils]], axis=0
-            )
+    unit = onehot(iota((chan, 2 * chan), 0) == iota((chan, 2 * chan), 1))
+    sides = []
+    for side in range(2):
+        even = onehot(col == side * chan + 2 * src)
+        odd = onehot(col == side * chan + 2 * src + 1)
+        upper = (dot(real, even) - dot(imag, odd)).astype(BF)
+        lower = (dot(real, odd) + dot(imag, even)).astype(BF)
+        blocks = {}
+        for a in range(kx):
+            for c in range(kz):
+                at = slice((a * kz + c) * coils, (a * kz + c + 1) * coils)
+                both = jnp.concatenate([upper[at], lower[at]], axis=0)
+                blocks[a, c] = dot(weave, both)
+        sides.append(blocks)
+    zero = jnp.zeros((chan, 2 * chan), F32)
+    for c in range(kz):
+        for x in range(planes):
             row = (c * planes + x) * chan
-            out_ref[row : row + chan, :] = dot(weave, both).astype(BF)
+            for q in range((planes + kx - 1) // 2):
+                at = slice(2 * q * chan, 2 * (q + 1) * chan)
+                left, right = 2 * q - x, 2 * q + 1 - x
+                value = sides[0].get((left, c), zero) + sides[1].get((right, c), zero)
+                fwd_ref[row : row + chan, at] = value.astype(BF)
+                left, right = x + kx - 1 - 2 * q, x + kx - 2 - 2 * q
+                pair = jnp.concatenate(
+                    [sides[0].get((left, c), zero), sides[0].get((right, c), zero)], axis=0
+                )
+                adj_ref[row : row + chan, at] = dot_t(unit, pair.astype(BF)).astype(BF)
 
 
 def stencil(weights, window, rows, up):
@@ -74,12 +84,14 @@
 
 def kernel(
     dims,
-    meta,
-    grid,
-    samples,
-    interp,
-    fwd_taps,
-    adj_taps,
+    line_ids,
+    read_ids,
+    counts,
+    grid_in,
+    samples_in,
+    interp_in,
+    real_in,
+    imag_in,
     grad,
     resid,
     ext,
@@ -103,13 +115,33 @@
     a_recv,
     b_send,
     b_recv,
+    grid,
+    samples,
+    interp,
+    taps_real,
+    taps_imag,
+    in_sem,
 ):
     slabs, tiles, phases, planes, rows_y, chan, depth, kx, kz, cap, reads = dims
     coils = chan // 2
     lines = planes * rows_y
     own = planes * chan
     slots = phases * cap
-    seg = interp.shape[2]
+    seg = interp_in.shape[2]
+    loads = [
+        pltpu.make_async_copy(src, dst, in_sem.at[i])
+        for i, (src, dst) in enumerate(
+            (
+                (grid_in, grid),
+                (interp_in, interp),
+                (real_in, taps_real),
+                (imag_in, taps_imag),
+                (samples_in, samples),
+            )
+        )
+    ]
+    for load in loads:
+        load.start()
     slab = lax.axis_index("phases")
     me = lax.axis_index("tiles")
 
@@ -127,6 +159,7 @@
     def _():
         pl.semaphore_signal(barrier, inc=1, device_id={"phases": slab + 1})
 
+    loads[0].wait()
     for p in range(phases):
         for x in range(planes):
             for y in range(rows_y):
@@ -151,6 +184,9 @@
     @pl.when(slab == slabs - 1)
     def _():
         phi[...] = jnp.zeros(phi.shape, BF)
+
+    for load in loads[1:]:
+        load.wait()
 
     rows_i = iota((chan, chan), 0)
     cols_i = iota((chan, chan), 1)
@@ -169,45 +205,45 @@
     peers = tiles - 1 + jnp.where(slab > 0, 1, 0) + jnp.where(slab < slabs - 1, 1, 0)
     pl.semaphore_wait(barrier, peers)
 
-    def halo(ref, index, right):
+    def halo(ref, index, right, p):
         if right:
             src, dst, target = (own, 2 * own), (0, own), me + 1
         else:
             src, dst, target = (own, 2 * own), (2 * own, 3 * own), me - 1
         return pltpu.make_async_remote_copy(
-            src_ref=ref.at[:, :, src[0] : src[1], :],
-            dst_ref=ref.at[:, :, dst[0] : dst[1], :],
+            src_ref=ref.at[p, :, src[0] : src[1], :],
+            dst_ref=ref.at[p, :, dst[0] : dst[1], :],
             send_sem=halo_send.at[index],
             recv_sem=halo_recv.at[index],
             device_id={"tiles": target},
         )
 
-    def start_halo(ref, index):
+    def start_halo(ref, index, p):
         @pl.when(me < tiles - 1)
         def _():
-            halo(ref, index, True).start()
+            halo(ref, index + 2 * p, True, p).start()
 
         @pl.when(me > 0)
         def _():
-            halo(ref, index + 1, False).start()
-
-    def wait_halo(ref, index):
+            halo(ref, index + 2 * p + 1, False, p).start()
+
+    def wait_halo(ref, index, p):
         @pl.when(me > 0)
         def _():
-            halo(ref, index, True).wait_recv()
+            halo(ref, index + 2 * p, True, p).wait_recv()
 
         @pl.when(me < tiles - 1)
         def _():
-            halo(ref, index + 1, False).wait_recv()
-
-    def end_halo(ref, index):
+            halo(ref, index + 2 * p + 1, False, p).wait_recv()
+
+    def end_halo(ref, index, p):
         @pl.when(me < tiles - 1)
         def _():
-            halo(ref, index, True).wait_send()
+            halo(ref, index + 2 * p, True, p).wait_send()
 
         @pl.when(me > 0)
         def _():
-            halo(ref, index + 1, False).wait_send()
+            halo(ref, index + 2 * p + 1, False, p).wait_send()
 
     def phase_copy(up):
         return pltpu.make_async_remote_copy(
@@ -218,16 +254,25 @@
             device_id={"phases": slab + 1 if up else slab - 1},
         )
 
-    start_halo(ext, 0)
+    @pl.when(slab < slabs - 1)
+    def _():
+        phase_copy(True).start()
+
+    @pl.when(slab > 0)
+    def _():
+        phase_copy(False).start()
+
+    for p in range(phases):
+        start_halo(ext, 0, p)
 
     def line_of(p, o, c):
-        return meta[p, o * cap + c]
+        return line_ids[p, 0, c, o]
 
     def read_of(p, o, c):
-        return meta[p, (tiles + o) * cap + c]
+        return read_ids[p, 0, c, o]
 
     def live_of(p, o, c):
-        return jnp.where(c < meta[p, 2 * tiles * cap + o], 1.0, 0.0)
+        return jnp.where(c < counts[p, 0, o], 1.0, 0.0)
 
     pad = snd.shape[1] - slots * coils
 
@@ -286,26 +331,17 @@
 
     fill(me, rcv)
 
-    @pl.when(slab < slabs - 1)
-    def _():
-        phase_copy(True).start()
-
-    @pl.when(slab > 0)
-    def _():
-        phase_copy(False).start()
-
-    build_matrix(fwd_taps, w_fwd, coils, kx, kz, planes, False)
-    build_matrix(adj_taps, w_adj, coils, kx, kz, planes, True)
-
-    wait_halo(ext, 0)
-    for p in range(phases):
+    build_matrices(taps_real, taps_imag, w_fwd, w_adj, planes)
+
+    for p in range(phases):
+        wait_halo(ext, 0, p)
         for y in range(rows_y):
             out = stencil(w_fwd[...], ext[p, y], own, False)
             for x in range(planes):
                 rest = out[x * chan : (x + 1) * chan] - grid[p, x, y]
                 grad[p, x, y] = -SPIRIT_WEIGHT * rest
                 ext2[p, y, own + x * chan : own + (x + 1) * chan, :] = rest.astype(BF)
-    start_halo(ext2, 2)
+        start_halo(ext2, 2 * phases, p)
 
     for p in range(phases):
         for r in range(reads):
@@ -377,8 +413,8 @@
                 bend = diff[p] - 2.0 * diff[p + 1] + diff[p + 2]
                 grad[p, x, y] = grad[p, x, y] + PHASE_WEIGHT * bend
 
-    wait_halo(ext2, 2)
-    for p in range(phases):
+    for p in range(phases):
+        wait_halo(ext2, 2 * phases, p)
         for y in range(rows_y):
             out = stencil(w_adj[...], ext2[p, y], own, True)
             for x in range(planes):
@@ -423,8 +459,9 @@
             woven = dot(weave, both).astype(BF)
             grad[p, x, y] = grad[p, x, y] + dot(woven, four)
 
-    end_halo(ext, 0)
-    end_halo(ext2, 2)
+    for p in range(phases):
+        end_halo(ext, 0, p)
+        end_halo(ext2, 2 * phases, p)
 
     @pl.when(slab < slabs - 1)
     def _():
@@ -463,17 +500,6 @@
     message = slots * coils + 16 * -(-slots // 16)
     lines = planes * rows_y
     width = (planes + kx - 1) * chan
-    meta = jnp.concatenate(
-        [
-            segment_line.reshape(phases, -1),
-            segment_readout.reshape(phases, -1),
-            segment_count.reshape(phases, -1),
-        ],
-        axis=1,
-    )
-    both = jnp.stack([kernel_real, kernel_imag])
-    fwd_taps = jnp.transpose(both, (2, 3, 0, 1, 4)).reshape(kz * coils, 2 * kx * coils)
-    adj_taps = jnp.transpose(both, (2, 4, 0, 1, 3)).reshape(kz * coils, 2 * kx * coils)
     dims = (slabs, tiles, phases, planes, rows_y, chan, depth, kx, kz, cap, reads)
     vmem = pl.BlockSpec(memory_space=pltpu.VMEM)
     dma = pltpu.SemaphoreType.DMA
@@ -483,7 +509,7 @@
             jax.ShapeDtypeStruct(kspace_grid.shape, F32),
             jax.ShapeDtypeStruct(samples.shape, F32),
         ),
-        in_specs=[pl.BlockSpec(memory_space=pltpu.SMEM)] + [vmem] * 5,
+        in_specs=[pl.BlockSpec(memory_space=pltpu.SMEM)] * 3 + [pl.BlockSpec(memory_space=pltpu.HBM)] * 5,
         out_specs=(vmem, vmem),
         scratch_shapes=[
             pltpu.VMEM((phases, rows_y, 3 * own, depth), BF),
@@ -499,19 +525,34 @@
             pltpu.VMEM((phases * lines, coils, 2 * seg), F32),
             pltpu.VMEM((kz * own, width), BF),
             pltpu.VMEM((kz * own, width), BF),
-            dma((4,)),
-            dma((4,)),
+            dma((4 * phases,)),
+            dma((4 * phases,)),
             dma((2,)),
             dma((2,)),
             dma((tiles,)),
             dma((tiles,)),
             dma((tiles,)),
             dma((tiles,)),
+            pltpu.VMEM(kspace_grid.shape, F32),
+            pltpu.VMEM(samples.shape, F32),
+            pltpu.VMEM(interp_matrix.shape, BF),
+            pltpu.VMEM(kernel_real.shape, BF),
+            pltpu.VMEM(kernel_imag.shape, BF),
+            dma((5,)),
         ],
         compiler_params=pltpu.CompilerParams(
-            collective_id=0, has_side_effects=True, vmem_limit_bytes=48 * 1024 * 1024
+            collective_id=0, has_side_effects=True, vmem_limit_bytes=58 * 1024 * 1024
         ),
-    )(meta, kspace_grid, samples, interp_matrix, fwd_taps, adj_taps)
+    )(
+        jnp.transpose(segment_line, (0, 1, 3, 2)),
+        jnp.transpose(segment_readout, (0, 1, 3, 2)),
+        segment_count,
+        kspace_grid,
+        samples,
+        interp_matrix,
+        kernel_real,
+        kernel_imag,
+    )
 
 
 def solution(mesh):

time: 48.3 us -> 45.8 us (0.948)
  local copies, waits for them, and re-layouts: 5.54 us -> 2.82 us
  Pallas kernels: 40.7 us -> 42.1 us
  other arithmetic: 1.09 us -> 0 us
    unnamed x16 -> x4, local copies, waits for them, and re-layouts: 4.38 us -> 2.82 us
    pallas_call x1, Pallas kernels: 40.7 us -> 42.1 us  [on_device(): pl.pallas_call(functools.partial(kernel, dims), out_shape=(jax.ShapeDtype...]
    reshape x6 -> x0, local copies, waits for them, and re-layouts: 1.15 us -> none  [the longest x2 0.6 us: on_device(): jnp.transpose(both, (2, 4, 0, 1, 3)).reshape(kz * coils, 2 * kx * coils)]
    transpose x1 -> x0, other arithmetic: 1.01 us -> none  [on_device(): jnp.transpose(both, (2, 4, 0, 1, 3)).reshape(kz * coils, 2 * kx * coils)]
where the time goes in v2:
time: 45.8 us; the launch traced here: 45.6 us
  Pallas kernels  42.1 us (92%)
  local copies, waits for them, and re-layouts  2.82 us (6%)
  between operations  0.65 us (1%)
    pallas_call x1, Pallas kernels, on_device(): pl.pallas_call(functools.partial(kernel, dims), out_shape=(jax.ShapeDtype...  42.1 us
    unnamed x4, local copies, waits for them, and re-layouts  2.82 us

profile of v2, /device:TPU:0, one launch (start us, length us, event | category | flops | bytes accessed | tf_op | source)
XLA Modules:
  0.0 45.6 jit_solution(14650818023044167671)
XLA Ops:
  0.6 42.1 %shard_map.95 = (f32[2,2,2,64,384]{4,3,2,1,0:T(8,128)}, f32[2,8,32,128]{3,2,1,0:T(8,128)}) custom-call(s32[2,1,2,16]{3,2,1,0:T(2,128)} %bitcast.2, s32[2,1,2,16]{3,2,1,0:T(2,128)} %bitcast.3, s32[2,1,16]{2,1,0:T(1,128)} %counts.1, f32[2,2,2,64,384]{4,3,2,1,0:T(8,128)} %grid_in.1, f32[2,8,32,128]{3,2,1,0:T(8,128)} %samples_in.1, ...), custom_call_target="tpu_custom_call" | custom-call | tf_op jit(solution)/shard_map/pallas_call | solution.py:506
  42.7 0.0 copy-start
  42.8 2.1 %copy.12 = f32[2,2,2,64,384]{4,3,2,1,0:T(8,128)} copy(f32[2,2,2,64,384]{4,3,2,1,0:T(8,128)} %get-tuple-element.4) | data formatting | bytes 1572864
  44.9 0.0 copy-done
  44.9 0.7 %copy.13 = f32[2,8,32,128]{3,2,1,0:T(8,128)} copy(f32[2,8,32,128]{3,2,1,0:T(8,128)S(1)} %copy-done) | data formatting | bytes 524288
Async XLA Ops:
  42.7 2.1 %copy-start = (f32[2,8,32,128]{3,2,1,0:T(8,128)S(1)}, f32[2,8,32,128]{3,2,1,0:T(8,128)}, u32[]{:S(2)}) copy-start(f32[2,8,32,128]{3,2,1,0:T(8,128)} %get-tuple-element.5) | copy-start | bytes 786436

commit v3 on v2

--- a/solution.py
+++ b/solution.py
@@ -325,7 +325,7 @@
 
     @pl.loop(1, tiles)
     def _(k):
-        o = lax.rem(me + k, tiles)
+        o = lax.rem(me + 1 + lax.rem(k + tiles // 2 - 2, tiles - 1), tiles)
         fill(o, snd)
         there(o).start()
 

time: 45.8 us -> 45.4 us (level)
  the two profiles are of different devices: /device:TPU:0 before, /device:TPU:25 now
where the time goes in v3:
time: 45.4 us; the launch traced here: 45.2 us
  Pallas kernels  41.8 us (92%)
  local copies, waits for them, and re-layouts  2.82 us (6%)
  between operations  0.65 us (1%)
    pallas_call x1, Pallas kernels, on_device(): pl.pallas_call(functools.partial(kernel, dims), out_shape=(jax.ShapeDtype...  41.8 us
    unnamed x4, local copies, waits for them, and re-layouts  2.82 us

profile of v3, /device:TPU:25, one launch (start us, length us, event | category | flops | bytes accessed | tf_op | source)
XLA Modules:
  0.0 45.2 jit_solution(1730280012715494846)
XLA Ops:
  0.6 41.8 %shard_map.95 = (f32[2,2,2,64,384]{4,3,2,1,0:T(8,128)}, f32[2,8,32,128]{3,2,1,0:T(8,128)}) custom-call(s32[2,1,2,16]{3,2,1,0:T(2,128)} %bitcast.2, s32[2,1,2,16]{3,2,1,0:T(2,128)} %bitcast.3, s32[2,1,16]{2,1,0:T(1,128)} %counts.1, f32[2,2,2,64,384]{4,3,2,1,0:T(8,128)} %grid_in.1, f32[2,8,32,128]{3,2,1,0:T(8,128)} %samples_in.1, ...), custom_call_target="tpu_custom_call" | custom-call | tf_op jit(solution)/shard_map/pallas_call | solution.py:506
  42.4 0.0 copy-start
  42.4 2.1 %copy.12 = f32[2,2,2,64,384]{4,3,2,1,0:T(8,128)} copy(f32[2,2,2,64,384]{4,3,2,1,0:T(8,128)} %get-tuple-element.4) | data formatting | bytes 1572864
  44.5 0.0 copy-done
  44.5 0.7 %copy.13 = f32[2,8,32,128]{3,2,1,0:T(8,128)} copy(f32[2,8,32,128]{3,2,1,0:T(8,128)S(1)} %copy-done) | data formatting | bytes 524288
Async XLA Ops:
  42.4 2.1 %copy-start = (f32[2,8,32,128]{3,2,1,0:T(8,128)S(1)}, f32[2,8,32,128]{3,2,1,0:T(8,128)}, u32[]{:S(2)}) copy-start(f32[2,8,32,128]{3,2,1,0:T(8,128)} %get-tuple-element.5) | copy-start | bytes 786436
